TPU v7x, 256 devices: a whole 4x4x8 slice. The times are simulated.
256 devices in a mesh: seq: 32 (over z, x), tp: 8 (over y, core).
Axes of the slice: x: 4, y: 4, z: 8, core: 2. Of those that a mesh axis runs over, the one named last changes fastest.
Arguments:
- queries: bfloat16 [2048, 2048], P('seq', 'tp'), may hold values from -4.5 to 4.5
- keys: bfloat16 [16384, 2048], P('seq', 'tp'), may hold values from -4.5 to 4.5
- values: bfloat16 [16384, 2048], P('seq', 'tp'), may hold values from -24 to 24
- visible: int32 [2048], replicated, may hold values from 12290 to 16384, as said below
- out_weight: bfloat16 [2048, 2048], P('tp'), may hold values from -0.125 to 0.125
- out_cotangent: bfloat16 [2048, 2048], P('seq', 'tp'), may hold values from -24 to 24
Outputs:
- projected: bfloat16 [2048, 2048], P('seq', 'tp')
- grad_queries: float32 [2048, 2048], P('seq', 'tp')
- grad_keys: float32 [16384, 2048], P('seq', 'tp')
- grad_values: float32 [16384, 2048], P('seq', 'tp')
Inputs may be any that keep to these rules, and one draw needn't show every extreme that they name: visible rises strictly with the latent index, by 1 or 2 from one latent to the next, and the last latent sees all 16384 tokens.
All inputs are finite; a program needn't handle non-finite values.
Results may differ from a plain program's by a relative error of at most 0.02.
Values may be sent and summed in bfloat16 or wider, within the bound.
A program may use at most 128 MiB of HBM per device.

v0:
```python
import math

import jax
import jax.numpy as jnp
from jax import lax
from jax.sharding import PartitionSpec as P

D = 2048
HEADS = 16


def body(queries, keys, values, visible, out_weight, out_cotangent):
    head_dim = D // HEADS
    own_rows, local_width = queries.shape
    local_heads = local_width // head_dim
    context_rows = keys.shape[0]
    score_scale = 1.0 / math.sqrt(head_dim)
    seq_index = lax.axis_index("seq")
    key_position = seq_index * context_rows + jnp.arange(context_rows, dtype=jnp.int32)
    all_queries = lax.all_gather(queries, "seq", axis=0, tiled=True)
    latent_rows = all_queries.shape[0]
    block_rows = min(512, latent_rows)
    block_count = latent_rows // block_rows
    query_heads = all_queries.reshape(latent_rows, local_heads, head_dim)
    key_heads = keys.reshape(context_rows, local_heads, head_dim)
    value_heads = values.reshape(context_rows, local_heads, head_dim)

    def block_scores(first_row):
        query_block = query_heads[first_row : first_row + block_rows]
        scores = (
            jnp.einsum("jhe,che->hjc", query_block, key_heads, preferred_element_type=jnp.float32)
            * score_scale
        )
        visible_mask = key_position[None, :] < visible[first_row : first_row + block_rows, None]
        return (scores, visible_mask[None])

    max_blocks = []
    for block_index in range(block_count):
        scores, visible_mask = block_scores(block_index * block_rows)
        max_blocks.append(jnp.max(jnp.where(visible_mask, scores, -1e30), axis=2))
    row_max = lax.pmax(jnp.concatenate(max_blocks, axis=1), "seq")

    def block_weights(first_row):
        scores, visible_mask = block_scores(first_row)
        maxima = row_max[:, first_row : first_row + block_rows, None]
        return jnp.exp(jnp.where(visible_mask, scores - maxima, -jnp.inf))

    numer_blocks = []
    total_blocks = []
    for block_index in range(block_count):
        weights = block_weights(block_index * block_rows)
        total_blocks.append(jnp.sum(weights, axis=2).T)
        numer_blocks.append(
            jnp.einsum(
                "hjc,che->jhe",
                weights.astype(jnp.bfloat16),
                value_heads,
                preferred_element_type=jnp.float32,
            )
        )
    numerator = jnp.concatenate(numer_blocks, axis=0).reshape(latent_rows, local_width)
    totals = jnp.concatenate(total_blocks, axis=0)
    numer_all, totals_all = lax.psum((numerator, totals), "seq")
    first_own = seq_index * own_rows
    numerator_own = lax.dynamic_slice_in_dim(numer_all, first_own, own_rows, 0)
    totals_own = lax.dynamic_slice_in_dim(totals_all, first_own, own_rows, 0)
    attended = (
        (numerator_own.reshape(own_rows, local_heads, head_dim) / totals_own[:, :, None])
        .astype(jnp.bfloat16)
        .reshape(own_rows, local_width)
    )
    head_terms = jnp.dot(attended, out_weight, preferred_element_type=jnp.float32)
    projected = lax.psum_scatter(
        head_terms.astype(jnp.bfloat16), "tp", scatter_dimension=1, tiled=True
    )
    cotangent_rows = lax.all_gather(out_cotangent, "tp", axis=1, tiled=True)
    grad_attended = jnp.dot(cotangent_rows, out_weight.T, preferred_element_type=jnp.float32)
    scaled_grad = (
        (grad_attended.reshape(own_rows, local_heads, head_dim) / totals_own[:, :, None])
        .astype(jnp.bfloat16)
        .reshape(own_rows, local_width)
    )
    grad_rows, output_rows = (
        lax.all_gather(scaled_grad, "seq", axis=0, tiled=True),
        lax.all_gather(attended, "seq", axis=0, tiled=True),
    )
    grad_heads = grad_rows.reshape(latent_rows, local_heads, head_dim)
    output_heads = output_rows.reshape(latent_rows, local_heads, head_dim)
    delta = jnp.sum(grad_heads.astype(jnp.float32) * output_heads.astype(jnp.float32), axis=2).T
    grad_keys = jnp.zeros((context_rows, local_heads, head_dim), jnp.float32)
    grad_values = jnp.zeros((context_rows, local_heads, head_dim), jnp.float32)
    query_blocks = []
    for block_index in range(block_count):
        first_row = block_index * block_rows
        weights = block_weights(first_row)
        grad_block = grad_heads[first_row : first_row + block_rows]
        grad_values = grad_values + jnp.einsum(
            "hjc,jhe->che",
            weights.astype(jnp.bfloat16),
            grad_block,
            preferred_element_type=jnp.float32,
        )
        grad_prob = jnp.einsum(
            "jhe,che->hjc", grad_block, value_heads, preferred_element_type=jnp.float32
        )
        grad_score = (
            weights * (grad_prob - delta[:, first_row : first_row + block_rows, None])
        ).astype(jnp.bfloat16)
        query_blocks.append(
            jnp.einsum("hjc,che->jhe", grad_score, key_heads, preferred_element_type=jnp.float32)
            * score_scale
        )
        grad_keys = (
            grad_keys
            + jnp.einsum(
                "hjc,jhe->che",
                grad_score,
                query_heads[first_row : first_row + block_rows],
                preferred_element_type=jnp.float32,
            )
            * score_scale
        )
    query_term = jnp.concatenate(query_blocks, axis=0).reshape(latent_rows, local_width)
    grad_queries = lax.psum_scatter(
        query_term.astype(jnp.bfloat16), "seq", scatter_dimension=0, tiled=True
    ).astype(jnp.float32)
    return (
        projected,
        grad_queries,
        grad_keys.reshape(context_rows, local_width),
        grad_values.reshape(context_rows, local_width),
    )


def solution(mesh):
    return jax.shard_map(
        body,
        mesh=mesh,
        in_specs=(
            P("seq", "tp"),
            P("seq", "tp"),
            P("seq", "tp"),
            P(),
            P("tp", None),
            P("seq", "tp"),
        ),
        out_specs=(P("seq", "tp"), P("seq", "tp"), P("seq", "tp"), P("seq", "tp")),
        check_vma=False,
    )
```

profile of v0, /device:TPU:2, one launch (start us, length us, event | category | flops | bytes accessed | tf_op | source)
XLA Modules:
  0.0 836.1 jit_solution(1668562604307579101)
XLA Ops:
  8.7 1.4 broadcast_compare_fusion.3
  10.1 78.7 %all-gather.4.cloned.1.call-done = bf16[2048,256]{1,0:T(8,128)(2,1)} async-done(((bf16[64,256]{1,0:T(8,128)(2,1)}), bf16[2048,256]{1,0:T(8,128)(2,1)}) %all-gather.4.cloned.1.call-update) | async-done | bytes 1048592 | tf_op jit(solution)/shard_map/all_gather | solution.py:20
  88.8 1.3 fusion.67
  91.3 1.9 select_reduce_fusion.3
  93.2 1.9 select_reduce_fusion.2
  95.2 1.9 select_reduce_fusion.1
  97.6 136.2 %pmax.7 = f32[2,2048]{1,0:T(2,128)S(1)} all-reduce(f32[2,2048]{1,0:T(2,128)S(1)} %pad_maximum_fusion.2), channel_id=1, replica_groups=mesh['seq'=32,'tp'=8] {'seq'}, use_global_device_ids=true, to_apply=%region_4.5 | all-reduce | flops 4096 | bytes 32768 | tf_op jit(solution)/shard_map/pmax | solution.py:41
  233.8 2.5 convolution_bitcast_fusion.3
  239.9 1.8 copy.143
  241.7 2.9 copy.144
  244.7 14.5 %all_gather.13 = bf16[64,2048]{1,0:T(8,128)(2,1)} all-gather(bf16[64,256]{1,0:T(8,128)(2,1)S(1)} %copy-done.48), channel_id=1, replica_groups=mesh['seq'=32,'tp'=8] {'tp'}, dimensions={1}, use_global_device_ids=true | all-gather | bytes 294912 | tf_op jit(solution)/shard_map/all_gather | solution.py:76
  259.3 2.8 fusion.11
  263.3 140.2 %psum.15 = f32[2048,2]{0,1:T(2,128)S(1)} all-reduce(f32[2048,2]{0,1:T(2,128)S(1)} %pad_maximum_fusion.3), channel_id=1, replica_groups=mesh['seq'=32,'tp'=8] {'seq'}, use_global_device_ids=true, to_apply=%region_10.11 | all-reduce | flops 4096 | bytes 32768 | tf_op jit(solution)/shard_map/psum | solution.py:63
  403.9 1.1 fusion.10
  405.0 1.5 fusion.39
  406.8 73.2 %all-gather.6.cloned.1.call-done = bf16[2048,256]{1,0:T(8,128)(2,1)} async-done(((bf16[64,256]{1,0:T(8,128)(2,1)}), bf16[2048,256]{1,0:T(8,128)(2,1)}) %all-gather.6.cloned.1.call-update) | async-done | bytes 1048592 | tf_op jit(solution)/shard_map/all_gather | solution.py:84
  480.0 1.3 fusion.66
  484.6 72.6 %all-gather.8.cloned.1.call-done = bf16[2048,256]{1,0:T(8,128)(2,1)} async-done(((bf16[64,256]{1,0:T(8,128)(2,1)}), bf16[2048,256]{1,0:T(8,128)(2,1)}) %all-gather.8.cloned.1.call-update) | async-done | bytes 1048592 | tf_op jit(solution)/shard_map/all_gather | solution.py:85
  557.2 1.8 convert_multiply_fusion
  558.9 2.1 mul.91
  561.1 4.7 reduce_sum.49
  566.5 1.1 copy.148
  568.0 2.7 multiply_convert_fusion
  575.9 1.1 pad_maximum_fusion.1
  577.0 2.3 copy.170
  579.2 2.3 copy.219
  581.9 2.5 fusion.62
  587.7 1.5 convolution_add_fusion
  589.3 2.1 copy.190
  592.8 1.7 convolution_add_fusion.5
  596.7 197.2 %reduce-scatter.7.cloned.1.call-done = bf16[64,256]{1,0:T(8,128)(2,1)} async-done(((bf16[2048,256]{1,0:T(8,128)(2,1)}), bf16[64,256]{1,0:T(8,128)(2,1)}) %reduce-scatter.7.cloned.1.call-update) | async-done | bytes 32784
  795.5 33.8 %reduce-scatter.5.cloned.1.call-done = bf16[64,256]{1,0:T(8,128)(2,1)} async-done(((bf16[64,2048]{1,0:T(8,128)(2,1)}), bf16[64,256]{1,0:T(8,128)(2,1)}) %reduce-scatter.5.cloned.1.call-update) | async-done | bytes 32784 | tf_op jit(solution)/shard_map/reduce_scatter | solution.py:73
  (158 shorter events, 27.0 us)
Async XLA Ops:
  7.2 396.7 %copy-start = (bf16[256,2048]{1,0:T(8,128)(2,1)S(1)}, bf16[256,2048]{1,0:T(8,128)(2,1)}, u32[]{:S(2)}) copy-start(bf16[256,2048]{1,0:T(8,128)(2,1)} %param.10) | copy-start | bytes 3145732
  7.2 81.6 %all-gather.4.cloned.1.call-start = ((), (), s32[]{:S(2)}) async-start(), calls=%async_computation.2 | async-start | bytes 1081344 | tf_op jit(solution)/shard_map/all_gather | solution.py:20
  7.9 397.1 %all-reduce.2.cloned.1.call-start = ((), (), s32[]{:S(2)}) async-start(), calls=%async_computation.3 | async-start | bytes 4194304 | tf_op jit(solution)/shard_map/psum | solution.py:63
  10.1 81.2 %copy-start.38 = (pred[512,512]{0,1:T(8,128)(4,1)}, pred[512,512]{0,1:T(8,128)(4,1)S(1)}, u32[]{:S(2)}) copy-start(pred[512,512]{0,1:T(8,128)(4,1)S(1)} %get-tuple-element.36) | copy-start | bytes 786436
  10.1 83.1 %copy-start.34 = (pred[512,512]{0,1:T(8,128)(4,1)}, pred[512,512]{0,1:T(8,128)(4,1)S(1)}, u32[]{:S(2)}) copy-start(pred[512,512]{0,1:T(8,128)(4,1)S(1)} %get-tuple-element.37) | copy-start | bytes 786436
  10.1 85.1 %copy-start.29 = (pred[512,512]{0,1:T(8,128)(4,1)}, pred[512,512]{0,1:T(8,128)(4,1)S(1)}, u32[]{:S(2)}) copy-start(pred[512,512]{0,1:T(8,128)(4,1)S(1)} %get-tuple-element.38) | copy-start | bytes 786436
  10.1 81.2 %copy-start.4 = (bf16[512,256]{1,0:T(8,128)(2,1)S(1)}, bf16[512,256]{1,0:T(8,128)(2,1)}, u32[]{:S(2)}) copy-start(bf16[512,256]{1,0:T(8,128)(2,1)} %param.7) | copy-start | bytes 786436
  90.2 3.1 copy-start.21
  90.3 4.8 copy-start.17
  90.5 4.7 copy-start.23
  97.6 139.6 %copy-start.5 = (f32[2,512,512]{1,2,0:T(8,128)}, f32[2,512,512]{1,2,0:T(8,128)S(1)}, u32[]{:S(2)}) copy-start(f32[2,512,512]{1,2,0:T(8,128)S(1)} %get-tuple-element.41) | copy-start | bytes 6291460
  233.8 2.5 copy-start.49
  241.7 3.0 copy-start.48
  244.7 14.6 %copy-start.13 = (f32[2,512,512]{1,2,0:T(8,128)S(1)}, f32[2,512,512]{1,2,0:T(8,128)}, u32[]{:S(2)}) copy-start(f32[2,512,512]{1,2,0:T(8,128)} %get-tuple-element.45) | copy-start | bytes 6291460
  244.7 235.3 %all-gather.6.cloned.1.call-start = ((), (), s32[]{:S(2)}) async-start(), calls=%async_computation.5 | async-start | bytes 1081344 | tf_op jit(solution)/shard_map/all_gather | solution.py:84
  259.2 2.8 copy-start.6
  259.2 3.0 copy-start.9
  259.2 3.0 copy-start.26
  259.2 3.1 copy-start.31
  262.3 141.5 %copy-start.40 = (bf16[64,2048]{1,0:T(8,128)(2,1)S(1)}, bf16[64,2048]{1,0:T(8,128)(2,1)}, u32[]{:S(2)}) copy-start(bf16[64,2048]{1,0:T(8,128)(2,1)} %all_gather.13) | copy-start | bytes 786436
  404.9 152.2 %all-gather.8.cloned.1.call-start = ((), (), s32[]{:S(2)}) async-start(), calls=%async_computation.6 | async-start | bytes 1081344 | tf_op jit(solution)/shard_map/all_gather | solution.py:85
  406.5 387.4 %reduce-scatter.7.cloned.1.call-start = ((), (), s32[]{:S(2)}) async-start(), calls=%async_computation.7 | async-start | bytes 1081344
  568.0 3.2 copy-start.10
  568.0 3.2 copy-start.32
  568.0 3.2 copy-start.43
  568.0 3.2 copy-start.50
  581.5 2.9 copy-start.37
  581.6 247.7 %reduce-scatter.5.cloned.1.call-start = ((), (), s32[]{:S(2)}) async-start(), calls=%async_computation.4 | async-start | bytes 294912 | tf_op jit(solution)/shard_map/reduce_scatter | solution.py:73
  581.8 2.6 copy-start.15
  581.8 2.6 copy-start.47
  587.7 3.6 copy-start.41
  589.3 3.1 copy-start.22
  (25 other events, 44.5 us)
Sparse Core Ops, SparseCore 0:
  10.6 78.1 all-gather.3
  244.8 155.1 all-reduce.1
  405.1 74.8 all-gather.5
  483.3 73.7 all-gather.7
  581.7 212.1 reduce-scatter.6
  797.0 32.2 reduce-scatter.4
where the time goes:
time: 837 us; the launch traced here: 836 us
  waiting for transfers between devices  456 us (54%)
  blocking collectives  291 us (35%)
  local copies, waits for them, and re-layouts  30.4 us (4%)
  matrix products  28.8 us (3%)
  between operations  14.8 us (2%)
  other arithmetic  14.3 us (2%)
    unnamed x7, waiting for transfers between devices  198 us
    psum x1, blocking collectives, body(): numer_all, totals_all = lax.psum((numerator, totals), 'seq')  140 us
    pmax x1, blocking collectives, body(): row_max = lax.pmax(jnp.concatenate(max_blocks, axis=1), 'seq')  136 us
    all_gather x1, waiting for transfers between devices, body(): all_queries = lax.all_gather(queries, 'seq', axis=0, tiled=True)  78.7 us
    all_gather x1, waiting for transfers between devices, body(): lax.all_gather(scaled_grad, 'seq', axis=0, tiled=True)  73.2 us
    all_gather x1, waiting for transfers between devices, body(): lax.all_gather(attended, 'seq', axis=0, tiled=True)  72.6 us
    reduce_scatter x1, waiting for transfers between devices, body(): lax.psum_scatter(head_terms.astype(jnp.bfloat16), 'tp', scatter_dimension...  33.8 us
  transfers between devices with their start and end apart: 6, of which 5 were waited for; matrix products, arithmetic and copies ran while one was open for 3% of the time, Pallas kernels for 0%

commit v1 on v0

v1 whole, which is shorter than its diff:
```python
import math

import jax
import jax.numpy as jnp
from jax import lax
from jax.experimental import pallas as pl
from jax.experimental.pallas import tpu as pltpu
from jax.sharding import PartitionSpec as P

HEAD = 128
NZ = 8
NX = 4
NT = 8
MESH = pl.DeviceIdType.MESH
F32 = jnp.float32
BF16 = jnp.bfloat16
NEG = -1e30
FLOOR = -1e29
SCALE = 1.0 / math.sqrt(HEAD)
EXP2_SCALE = SCALE / math.log(2.0)
LAST_LAST = (((1,), (1,)), ((), ()))


def dot(a, b):
    return jnp.dot(a, b, preferred_element_type=F32)


def dot_t(a, b):
    return lax.dot_general(a, b, LAST_LAST, preferred_element_type=F32)


def kernel(
    q_ref, k_ref, v_ref, vis_ref, wout_ref, cot_ref,
    proj_ref, gq_ref, gk_ref, gv_ref,
    qa, ga, ct, kt, vt, w, dp, sb, sz, sx, fin,
    nb, db, nx, dx, ns, ds, nz, dz, pt, pr,
    ct_s, ct_r, qz_s, qz_r, qx_s, qx_r, gz_s, gz_r, gx_s, gx_r,
    sz_s, sz_r, sx_s, sx_r, fz_s, fz_r,
    nx_s, nx_r, dx_s, dx_r, nz_s, nz_r, dz_s, dz_r, pt_s, pt_r,
):
    seq = lax.axis_index("seq")
    tp = lax.axis_index("tp")
    z0 = seq // NX
    x0 = lax.rem(seq, NX)
    rows = q_ref.shape[0]
    ctx = k_ref.shape[0]
    block = NX * rows
    heads = q_ref.shape[1] // HEAD

    def z_at(i):
        return lax.rem(z0 + i, NZ)

    def z_from(i):
        return lax.rem(z0 + NZ - i, NZ)

    def x_at(i):
        return lax.rem(x0 + i, NX)

    def t_at(i):
        return lax.rem(tp + i, NT)

    def z_dev(i):
        return {"seq": z_at(i) * NX + x0}

    def x_dev(i):
        return {"seq": z0 * NX + x_at(i)}

    def t_dev(i):
        return {"tp": t_at(i)}

    def remote(src, dst, send, recv, device):
        return pltpu.make_async_remote_copy(
            src_ref=src, dst_ref=dst, send_sem=send, recv_sem=recv,
            device_id=device, device_id_type=MESH,
        )

    def cols(h):
        return pl.ds(h * HEAD, HEAD)

    barrier = pltpu.get_barrier_semaphore()
    for count, device in ((NZ, z_dev), (NX, x_dev), (NT, t_dev)):
        @pl.loop(1, count)
        def _(i, device=device):
            pl.semaphore_signal(barrier, inc=1, device_id=device(i), device_id_type=MESH)

    for h in range(heads):
        qa[z0, x0, h] = q_ref[:, cols(h)]
    ct[tp] = cot_ref[...]
    pl.semaphore_wait(barrier, NZ + NX + NT - 3)

    def ct_copy(i):
        return remote(ct.at[tp], ct.at[tp], ct_s.at[i], ct_r.at[i], t_dev(i))

    def z_copy(buf, send, recv, i):
        return remote(buf.at[z0, x0], buf.at[z0, x0], send.at[i], recv.at[i], z_dev(i))

    def x_copy(buf, send, recv, b, i):
        return remote(buf.at[b, x0], buf.at[b, x0], send.at[b, i], recv.at[b, i], x_dev(i))

    @pl.loop(1, NT)
    def _(i):
        ct_copy(i).start()

    @pl.loop(1, NZ)
    def _(i):
        z_copy(qa, qz_s, qz_r, i).start()

    @pl.loop(1, NX)
    def _(i):
        x_copy(qa, qx_s, qx_r, z0, i).start()

    for h in range(heads):
        kt[h] = k_ref[:, cols(h)].astype(F32).T.astype(BF16)
        vt[h] = v_ref[:, cols(h)].astype(F32).T.astype(BF16)
    gk_ref[...] = jnp.zeros_like(gk_ref)
    gv_ref[...] = jnp.zeros_like(gv_ref)

    @pl.loop(1, NT)
    def _(i):
        ct_copy(i).wait_recv()

    width = cot_ref.shape[1]
    for h in range(heads):
        total = jnp.zeros((rows, HEAD), F32)
        for t in range(NT):
            total += dot_t(ct[t], wout_ref[pl.ds(h * HEAD, HEAD), t * width : (t + 1) * width])
        ga[z0, x0, h] = total.astype(BF16)

    @pl.loop(1, NZ)
    def _(i):
        z_copy(ga, gz_s, gz_r, i).start()

    @pl.loop(1, NX)
    def _(i):
        x_copy(ga, gx_s, gx_r, z0, i).start()

    @pl.loop(1, NZ)
    def _(i):
        z_copy(qa, qz_s, qz_r, i).wait_recv()

        @pl.loop(1, NX)
        def _(j):
            x_copy(qa, qx_s, qx_r, z_from(i), j).start()

    @pl.loop(1, NZ)
    def _(i):
        z_copy(ga, gz_s, gz_r, i).wait_recv()

        @pl.loop(1, NX)
        def _(j):
            x_copy(ga, gx_s, gx_r, z_from(i), j).start()

    def stat_copy(i):
        return remote(sb.at[z_at(i)], sz.at[z0], sz_s.at[i], sz_r.at[i], z_dev(i))

    position = seq * ctx + lax.broadcasted_iota(jnp.int32, (ctx, 1), 0)

    @pl.loop(0, NZ)
    def _(i):
        b = z_from(i)

        @pl.loop(1, NX)
        def _(j):
            x_copy(qa, qx_s, qx_r, b, j).wait_recv()
            x_copy(ga, gx_s, gx_r, b, j).wait_recv()

        seen = position < vis_ref[b]
        stats = []
        for h in range(heads):
            query = qa[b, :, h].reshape(block, HEAD)
            grad = ga[b, :, h].reshape(block, HEAD)
            score = jnp.where(seen, dot_t(k_ref[:, cols(h)], query), NEG)
            top = jnp.maximum(jnp.max(score, axis=0, keepdims=True), FLOOR)
            weight = jnp.exp2((score - top) * EXP2_SCALE)
            prob = dot_t(v_ref[:, cols(h)], grad)
            w[h, b] = weight
            dp[h, b] = prob
            stats += [
                top,
                jnp.sum(weight, axis=0, keepdims=True),
                jnp.sum(weight * prob, axis=0, keepdims=True),
            ]
        stats.append(jnp.zeros((8 - len(stats), block), F32))
        sb[b] = jnp.concatenate(stats, axis=0)

        @pl.when(i > 0)
        def _():
            stat_copy(NZ - i).start()

    sz[z0] = sb[z0]

    @pl.loop(1, NZ)
    def _(i):
        stat_copy(i).wait_recv()

    def merged(ref):
        out = []
        for h in range(heads):
            tops = ref[:, 3 * h]
            top = jnp.max(tops, axis=0, keepdims=True)
            factor = jnp.exp2((tops - top) * EXP2_SCALE)
            out += [
                top,
                jnp.sum(ref[:, 3 * h + 1] * factor, axis=0, keepdims=True),
                jnp.sum(ref[:, 3 * h + 2] * factor, axis=0, keepdims=True),
            ]
        return out

    pad = jnp.zeros((8 - 3 * heads, block), F32)
    sx[x0] = jnp.concatenate(merged(sz) + [pad], axis=0)

    def stat_x_copy(i):
        return remote(sx.at[x0], sx.at[x0], sx_s.at[i], sx_r.at[i], x_dev(i))

    @pl.loop(1, NX)
    def _(i):
        stat_x_copy(i).start()

    @pl.loop(1, NX)
    def _(i):
        stat_x_copy(i).wait_recv()

    whole = merged(sx)
    final = []
    for h in range(heads):
        top, total, product = whole[3 * h : 3 * h + 3]
        final += [top * EXP2_SCALE + jnp.log2(total), product / total]
    final.append(jnp.zeros((8 - len(final), block), F32))
    fin[z0] = jnp.concatenate(final, axis=0)

    def fin_copy(i):
        return remote(fin.at[z0], fin.at[z0], fz_s.at[i], fz_r.at[i], z_dev(i))

    @pl.loop(1, NZ)
    def _(i):
        fin_copy(i).start()

    def nx_copy(b, i):
        return remote(nb.at[b, x_at(i)], nx.at[b, x0], nx_s.at[b, i], nx_r.at[b, i], x_dev(i))

    def dx_copy(b, i):
        return remote(db.at[b, x_at(i)], dx.at[b, x0], dx_s.at[b, i], dx_r.at[b, i], x_dev(i))

    @pl.loop(0, NZ)
    def _(i):
        b = z_from(i)

        @pl.when(i > 0)
        def _():
            fin_copy(i).wait_recv()

        for h in range(heads):
            log_total = fin[b, 2 * h : 2 * h + 1]
            factor = jnp.exp2(sb[b, 3 * h : 3 * h + 1] * EXP2_SCALE - log_total)
            weight = w[h, b] * factor
            w[h, b] = weight
            low = weight.astype(BF16)
            term = dot(vt[h], low).T.astype(BF16)
            nb[b, :, h] = term.reshape(NX, rows, HEAD)
            gv_ref[:, cols(h)] += dot(low, ga[b, :, h].reshape(block, HEAD))

        @pl.loop(1, NX)
        def _(j):
            nx_copy(b, j).start()

    @pl.loop(0, NZ)
    def _(i):
        b = z_from(i)
        for h in range(heads):
            delta = fin[b, 2 * h + 1 : 2 * h + 2]
            low = (w[h, b] * (dp[h, b] - delta)).astype(BF16)
            term = (dot(kt[h], low) * SCALE).T.astype(BF16)
            db[b, :, h] = term.reshape(NX, rows, HEAD)
            gk_ref[:, cols(h)] += dot(low, qa[b, :, h].reshape(block, HEAD))

        @pl.loop(1, NX)
        def _(j):
            dx_copy(b, j).start()

    gk_ref[...] = gk_ref[...] * SCALE

    def nz_copy(i):
        return remote(ns.at[z_at(i)], nz.at[z0], nz_s.at[i], nz_r.at[i], z_dev(i))

    def dz_copy(i):
        return remote(ds.at[z_at(i)], dz.at[z0], dz_s.at[i], dz_r.at[i], z_dev(i))

    def reduce_x(own, got, out, x_copies, z_copies):
        @pl.loop(0, NZ)
        def _(i):
            b = z_from(i)

            @pl.loop(1, NX)
            def _(j):
                x_copies(b, j).wait_recv()

            total = own[b, x0].astype(F32)
            for j in range(1, NX):
                total += got[b, x_at(j)].astype(F32)
            out[b] = total.astype(BF16)

            @pl.when(i > 0)
            def _():
                z_copies(NZ - i).start()

    def reduce_z(own, got, z_copies):
        @pl.loop(1, NZ)
        def _(i):
            z_copies(i).wait_recv()

        got[z0] = own[z0]
        total = got[0].astype(F32)
        for j in range(1, NZ):
            total += got[j].astype(F32)
        return total

    reduce_x(nb, nx, ns, nx_copy, nz_copy)
    attended = reduce_z(ns, nz, nz_copy).astype(BF16)

    def pt_copy(i):
        return remote(pt.at[t_at(i)], pr.at[tp], pt_s.at[i], pt_r.at[i], t_dev(i))

    for t in range(NT):
        term = jnp.zeros((rows, width), F32)
        for h in range(heads):
            term += dot(attended[h], wout_ref[pl.ds(h * HEAD, HEAD), t * width : (t + 1) * width])
        pt[t] = term.astype(BF16)

    @pl.loop(1, NT)
    def _(i):
        pt_copy(i).start()

    reduce_x(db, dx, ds, dx_copy, dz_copy)

    @pl.loop(1, NT)
    def _(i):
        pt_copy(i).wait_recv()

    pr[tp] = pt[tp]
    total = pr[0].astype(F32)
    for t in range(1, NT):
        total += pr[t].astype(F32)
    proj_ref[...] = total.astype(BF16)

    grad = reduce_z(ds, dz, dz_copy)
    for h in range(heads):
        gq_ref[:, cols(h)] = grad[h]

    @pl.loop(1, NT)
    def _(i):
        ct_copy(i).wait_send()
        pt_copy(i).wait_send()

    @pl.loop(1, NZ)
    def _(i):
        z_copy(qa, qz_s, qz_r, i).wait_send()
        z_copy(ga, gz_s, gz_r, i).wait_send()
        stat_copy(i).wait_send()
        fin_copy(i).wait_send()
        nz_copy(i).wait_send()
        dz_copy(i).wait_send()

    @pl.loop(1, NX)
    def _(j):
        stat_x_copy(j).wait_send()

        @pl.loop(0, NZ)
        def _(b):
            x_copy(qa, qx_s, qx_r, b, j).wait_send()
            x_copy(ga, gx_s, gx_r, b, j).wait_send()
            nx_copy(b, j).wait_send()
            dx_copy(b, j).wait_send()


def body(queries, keys, values, visible, out_weight, out_cotangent):
    rows, width = queries.shape
    ctx = keys.shape[0]
    heads = width // HEAD
    block = NX * rows
    vmem = pl.BlockSpec(memory_space=pltpu.VMEM)
    sem = pltpu.SemaphoreType.DMA
    return pl.pallas_call(
        kernel,
        out_shape=(
            jax.ShapeDtypeStruct((rows, width), BF16),
            jax.ShapeDtypeStruct((rows, width), F32),
            jax.ShapeDtypeStruct((ctx, width), F32),
            jax.ShapeDtypeStruct((ctx, width), F32),
        ),
        in_specs=[vmem] * 6,
        out_specs=[vmem] * 4,
        scratch_shapes=[
            pltpu.VMEM((NZ, NX, heads, rows, HEAD), BF16),
            pltpu.VMEM((NZ, NX, heads, rows, HEAD), BF16),
            pltpu.VMEM((NT, rows, width), BF16),
            pltpu.VMEM((heads, HEAD, ctx), BF16),
            pltpu.VMEM((heads, HEAD, ctx), BF16),
            pltpu.VMEM((heads, NZ, ctx, block), F32),
            pltpu.VMEM((heads, NZ, ctx, block), F32),
            pltpu.VMEM((NZ, 8, block), F32),
            pltpu.VMEM((NZ, 8, block), F32),
            pltpu.VMEM((NX, 8, block), F32),
            pltpu.VMEM((NZ, 8, block), F32),
            pltpu.VMEM((NZ, NX, heads, rows, HEAD), BF16),
            pltpu.VMEM((NZ, NX, heads, rows, HEAD), BF16),
            pltpu.VMEM((NZ, NX, heads, rows, HEAD), BF16),
            pltpu.VMEM((NZ, NX, heads, rows, HEAD), BF16),
            pltpu.VMEM((NZ, heads, rows, HEAD), BF16),
            pltpu.VMEM((NZ, heads, rows, HEAD), BF16),
            pltpu.VMEM((NZ, heads, rows, HEAD), BF16),
            pltpu.VMEM((NZ, heads, rows, HEAD), BF16),
            pltpu.VMEM((NT, rows, width), BF16),
            pltpu.VMEM((NT, rows, width), BF16),
            sem((NT,)), sem((NT,)),
            sem((NZ,)), sem((NZ,)), sem((NZ, NX)), sem((NZ, NX)),
            sem((NZ,)), sem((NZ,)), sem((NZ, NX)), sem((NZ, NX)),
            sem((NZ,)), sem((NZ,)), sem((NX,)), sem((NX,)), sem((NZ,)), sem((NZ,)),
            sem((NZ, NX)), sem((NZ, NX)), sem((NZ, NX)), sem((NZ, NX)),
            sem((NZ,)), sem((NZ,)), sem((NZ,)), sem((NZ,)),
            sem((NT,)), sem((NT,)),
        ],
        compiler_params=pltpu.CompilerParams(
            collective_id=0, has_side_effects=True, vmem_limit_bytes=56 * 2**20
        ),
    )(queries, keys, values, visible.reshape(NZ, 1, block), out_weight, out_cotangent)


def solution(mesh):
    return jax.shard_map(
        body,
        mesh=mesh,
        in_specs=(
            P("seq", "tp"),
            P("seq", "tp"),
            P("seq", "tp"),
            P(),
            P("tp", None),
            P("seq", "tp"),
        ),
        out_specs=(P("seq", "tp"), P("seq", "tp"), P("seq", "tp"), P("seq", "tp")),
        check_vma=False,
    )
```

time: 837 us -> 86.2 us (0.10)
  waiting for transfers between devices: 456 us -> 0 us
  blocking collectives: 291 us -> 0 us
  Pallas kernels: 0 us -> 80.6 us
  matrix products: 28.8 us -> 0 us
  local copies, waits for them, and re-layouts: 30.4 us -> 4.76 us
  other arithmetic: 14.3 us -> 0 us
  between operations: 14.8 us -> 0.65 us
    all_gather x3 -> x0, waiting for transfers between devices: 224 us -> none  [the longest x1 78.7 us: body(): all_queries = lax.all_gather(queries, 'seq', axis=0, tiled=True)]
    unnamed x7 -> x0, waiting for transfers between devices: 198 us -> none
    psum x1 -> x0, blocking collectives: 140 us -> none  [body(): numer_all, totals_all = lax.psum((numerator, totals), 'seq')]
    pmax x1 -> x0, blocking collectives: 136 us -> none  [body(): row_max = lax.pmax(jnp.concatenate(max_blocks, axis=1), 'seq')]
    pallas_call x0 -> x1, Pallas kernels: none -> 80.6 us  [body(): pl.pallas_call(kernel, out_shape=(jax.ShapeDtypeStruct((rows, width), BF1...]
    reduce_scatter x1 -> x0, waiting for transfers between devices: 33.8 us -> none  [body(): lax.psum_scatter(head_terms.astype(jnp.bfloat16), 'tp', scatter_dimension...]
    dot_general x26 -> x0, matrix products: 28.8 us -> none  [the longest x4 6.21 us: block_scores(): jnp.einsum('jhe,che->hjc', query_block, key_heads, preferred_element_type...]
    all_gather x1 -> x0, blocking collectives: 14.5 us -> none  [body(): cotangent_rows = lax.all_gather(out_cotangent, 'tp', axis=1, tiled=True)]
  transfers between devices with their start and end apart: 6 -> 0, of which waited for: 5 -> 0; matrix products, arithmetic and copies ran while one was open for 3% -> 0% of each run, Pallas kernels for 0% -> 0%
where the time goes in v1:
time: 86.2 us; the launch traced here: 86 us
  Pallas kernels  80.6 us (94%)
  local copies, waits for them, and re-layouts  4.76 us (6%)
    pallas_call x1, Pallas kernels, body(): pl.pallas_call(kernel, out_shape=(jax.ShapeDtypeStruct((rows, width), BF1...  80.6 us
    unnamed x8, local copies, waits for them, and re-layouts  4.76 us

profile of v1, /device:TPU:2, one launch (start us, length us, event | category | flops | bytes accessed | tf_op | source)
XLA Modules:
  0.0 86.0 jit_solution(15589180868105376720)
XLA Ops:
  0.6 80.6 %shard_map.93 = (bf16[64,256]{1,0:T(8,128)(2,1)}, f32[64,256]{1,0:T(8,128)}, f32[512,256]{1,0:T(8,128)}, f32[512,256]{1,0:T(8,128)}) custom-call(bf16[64,256]{1,0:T(8,128)(2,1)} %q_ref.1, bf16[512,256]{1,0:T(8,128)(2,1)} %k_ref.1, bf16[512,256]{1,0:T(8,128)(2,1)} %v_ref.1, s32[8,1,256]{2,1,0:T(1,128)} %bitcast.1, bf16[256,2048]{1,0:T(8,128)(2,1)} %wout_ref.1, ...), custom_call_target="tpu_custom_call" | custom-call | tf_op jit(solution)/shard_map/pallas_call | solution.py:382
  81.3 0.0 copy-start.1
  81.3 1.4 %copy.14 = bf16[64,256]{1,0:T(8,128)(2,1)} copy(bf16[64,256]{1,0:T(8,128)(2,1)} %get-tuple-element.8) | data formatting | bytes 65536
  82.7 0.0 copy-done.1
  82.7 0.6 copy.15
  83.3 0.0 copy-start
  83.3 1.9 %copy.16 = f32[512,256]{1,0:T(8,128)} copy(f32[512,256]{1,0:T(8,128)} %get-tuple-element.10) | data formatting | bytes 1048576
  85.2 0.0 copy-done
  85.2 0.8 copy.17
Async XLA Ops:
  81.3 1.4 %copy-start.1 = (f32[64,256]{1,0:T(8,128)S(1)}, f32[64,256]{1,0:T(8,128)}, u32[]{:S(2)}) copy-start(f32[64,256]{1,0:T(8,128)} %get-tuple-element.9) | copy-start | bytes 196612
  83.3 1.9 %copy-start = (f32[512,256]{1,0:T(8,128)S(1)}, f32[512,256]{1,0:T(8,128)}, u32[]{:S(2)}) copy-start(f32[512,256]{1,0:T(8,128)} %get-tuple-element.11) | copy-start | bytes 1572868

commit v2 on v1

v2 whole, which is shorter than its diff:
```python
import math

import jax
import jax.numpy as jnp
from jax import lax
from jax.experimental import pallas as pl
from jax.experimental.pallas import tpu as pltpu
from jax.sharding import PartitionSpec as P

HEAD = 128
NZ = 8
NX = 4
NT = 8
MESH = pl.DeviceIdType.MESH
F32 = jnp.float32
BF16 = jnp.bfloat16
NEG = -1e30
FLOOR = -1024.0
LEVEL_ROWS = 16
NEAR = (1, 7, 2, 6, 3, 5, 4)
CHAINS = ((0, 1, 4), (0, -1, 3), (1, 1, 3), (1, -1, 4))
SCALE = 1.0 / math.sqrt(HEAD)
EXP2_SCALE = SCALE / math.log(2.0)
LAST_LAST = (((1,), (1,)), ((), ()))


def dot(a, b):
    return jnp.dot(a, b, preferred_element_type=F32)


def dot_t(a, b):
    return lax.dot_general(a, b, LAST_LAST, preferred_element_type=F32)


def kernel(
    q_hbm, k_hbm, v_hbm, vis_hbm, wout_hbm, cot_hbm,
    proj_ref, gq_ref, gk_ref, gv_ref,
    k_ref, v_ref, vis_ref, wout_ref, in_s,
    qa, ga, ct, kt, vt, w, dp, nu, sb, sz, sx, fin,
    ring_out, ring_in, nb, nx, db, dx, ds, dz, pt, pr,
    ct_s, ct_r, qx_s, qx_r, qz_s, qz_r, gz_s, gz_r, gx_s, gx_r,
    sz_s, sz_r, sx_s, sx_r, fz_s, fz_r,
    rn_s, rn_r, nx_s, nx_r, dx_s, dx_r, dz_s, dz_r, pt_s, pt_r,
):
    seq = lax.axis_index("seq")
    tp = lax.axis_index("tp")
    z0 = seq // NX
    x0 = lax.rem(seq, NX)
    rows, width = q_hbm.shape
    ctx = k_hbm.shape[0]
    block = NX * rows
    heads = width // HEAD

    def z_at(i):
        return lax.rem(z0 + i, NZ)

    def z_from(i):
        return lax.rem(z0 + NZ - i, NZ)

    def x_at(i):
        return lax.rem(x0 + i, NX)

    def t_at(i):
        return lax.rem(tp + i, NT)

    def z_dev(i):
        return {"seq": z_at(i) * NX + x0}

    def x_dev(i):
        return {"seq": z0 * NX + x_at(i)}

    def t_dev(i):
        return {"tp": t_at(i)}

    def remote(src, dst, send, recv, device):
        return pltpu.make_async_remote_copy(
            src_ref=src, dst_ref=dst, send_sem=send, recv_sem=recv,
            device_id=device, device_id_type=MESH,
        )

    def cols(h):
        return pl.ds(h * HEAD, HEAD)

    def take(ref, sem):
        remote(ref, ref, sem, sem, {"tp": tp}).wait_recv()

    def sent(ref, sem):
        remote(ref, ref, sem, sem, {"tp": tp}).wait_send()

    def but_one(ref):
        return ref.at[pl.ds(0, ref.shape[0] - 1)]

    def each(count, action):
        @pl.loop(1, count)
        def _(i):
            action(i)

    loads = [
        pltpu.make_async_copy(src, dst, in_s.at[i])
        for i, (src, dst) in enumerate(
            [(q_hbm.at[:, cols(h)], qa.at[z0, h, x0]) for h in range(heads)]
            + [(cot_hbm, ct.at[tp]), (k_hbm, k_ref), (v_hbm, v_ref), (wout_hbm, wout_ref), (vis_hbm, vis_ref)]
        )
    ]
    for load in loads:
        load.start()

    barrier = pltpu.get_barrier_semaphore()
    for count, device in ((NZ, z_dev), (NX, x_dev), (NT, t_dev)):
        @pl.loop(1, count)
        def _(i, device=device):
            pl.semaphore_signal(barrier, inc=1, device_id=device(i), device_id_type=MESH)

    for load in loads[: heads + 1]:
        load.wait()
    pl.semaphore_wait(barrier, NZ + NX + NT - 3)

    def ct_copy(i):
        return remote(ct.at[tp], ct.at[tp], ct_s, ct_r, t_dev(i))

    def qx_copy(i):
        return remote(qa.at[z0, :, x0], qa.at[z0, :, x0], qx_s, qx_r, x_dev(i))

    def qz_copy(chain, n):
        h, sign, _ = CHAINS[chain]
        part = qa.at[z_from(sign * (n - 1)), h]
        return remote(part, part, qz_s.at[h], qz_r.at[chain, n - 1], z_dev(NZ + sign))

    def gz_copy(i):
        return remote(ga.at[z0, :, x0], ga.at[z0, :, x0], gz_s, gz_r.at[i], z_dev(i))

    def gx_copy(b, i):
        return remote(ga.at[b, :, x0], ga.at[b, :, x0], gx_s, gx_r.at[b], x_dev(i))

    each(NT, lambda i: ct_copy(i).start())
    each(NX, lambda i: qx_copy(i).start())

    for load in loads[heads + 1 :]:
        load.wait()
    for h in range(heads):
        kt[h] = k_ref[:, cols(h)].astype(F32).T.astype(BF16)
        vt[h] = v_ref[:, cols(h)].astype(F32).T.astype(BF16)

    take(qa.at[0, :, pl.ds(0, NX - 1)], qx_r)
    for chain in range(len(CHAINS)):
        qz_copy(chain, 1).start()

    sb[...] = jnp.zeros_like(sb)
    gk_ref[...] = jnp.zeros_like(gk_ref)
    gv_ref[...] = jnp.zeros_like(gv_ref)

    take(but_one(ct), ct_r)
    for h in range(heads):
        total = jnp.zeros((rows, HEAD), F32)
        for t in range(NT):
            total += dot_t(ct[t], wout_ref[pl.ds(h * HEAD, HEAD), t * width : (t + 1) * width])
        ga[z0, h, x0] = total.astype(BF16)
    each(NX, lambda i: gx_copy(z0, i).start())
    for i in NEAR:
        gz_copy(i).start()

    position = seq * ctx + lax.broadcasted_iota(jnp.int32, (ctx, 1), 0)

    def weigh(b):
        seen = position < vis_ref[b]
        for h in range(heads):
            score = jnp.where(seen, dot_t(k_ref[:, cols(h)], qa[b, h].reshape(block, HEAD)), NEG)
            top = jnp.max(score, axis=0, keepdims=True) * EXP2_SCALE
            level = jnp.ceil(jnp.maximum(top, FLOOR) * 0.25) * 4.0
            weight = jnp.exp2(score * EXP2_SCALE - level)
            w[h, b] = weight
            nu[h, b] = dot(vt[h], weight.astype(BF16))
            sb[b, pl.ds(3 * h, 1)] = level
            sb[b, pl.ds(3 * h + 1, 1)] = jnp.sum(weight, axis=0, keepdims=True)

    def pass_on(i):
        gz_copy(i).wait_recv()
        each(NX, lambda j: gx_copy(z_from(i), j).start())

    @pl.loop(1, NZ // 2 + 1)
    def _(n):
        for chain, (_, _, hops) in enumerate(CHAINS):
            @pl.when(n <= hops)
            def _(chain=chain):
                qz_copy(chain, n).wait_recv()

            @pl.when(n < hops)
            def _(chain=chain):
                qz_copy(chain, n + 1).start()

        @pl.when(n == 1)
        def _():
            for i in NEAR[:4]:
                pass_on(i)

        @pl.when(n == 2)
        def _():
            for i in NEAR[4:]:
                pass_on(i)

        weigh(z_from(n - 1))

        @pl.when(n > 1)
        def _():
            weigh(z_at(n - 1))

    weigh(z_at(NZ // 2))

    def ring_slot(chain, n):
        return n - 1 + CHAINS[chain - 1][2] * (chain % 2)

    def ring_copy(chain, n):
        h, sign, _ = CHAINS[chain]
        slot = ring_slot(chain, n)
        return remote(
            ring_out.at[h, slot], ring_in.at[h, slot],
            rn_s.at[h], rn_r.at[h, slot], z_dev(NZ + sign),
        )

    def arrived(chain, n):
        ring_copy(chain, n).wait_recv()
        h, slot = CHAINS[chain][0], ring_slot(chain, n)
        return (
            ring_in[h, slot, pl.ds(0, HEAD)].astype(F32),
            ring_in[h, slot, pl.ds(HEAD, LEVEL_ROWS)].astype(F32)[:1],
        )

    def own_part(h, b):
        return nu[h, b], sb[b, pl.ds(3 * h, 1)]

    def joined(parts):
        level = parts[0][1]
        for _, other in parts[1:]:
            level = jnp.maximum(level, other)
        total = sum(part * jnp.exp2(other - level) for part, other in parts)
        return total, level

    def ring_step(chain, n):
        h, sign, hops = CHAINS[chain]
        parts = [own_part(h, z_at(NZ + sign * n))]
        if n < hops:
            parts.append(arrived(chain, n + 1))
        total, level = joined(parts)
        slot = ring_slot(chain, n)
        ring_out[h, slot, pl.ds(0, HEAD)] = total.astype(BF16)
        ring_out[h, slot, pl.ds(HEAD, LEVEL_ROWS)] = jnp.broadcast_to(level, (LEVEL_ROWS, block)).astype(BF16)
        ring_copy(chain, n).start()

    for chain, (_, _, hops) in enumerate(CHAINS):
        ring_step(chain, hops)

    def stat_copy(i):
        return remote(sb.at[z_at(i)], sz.at[z0], sz_s, sz_r, z_dev(i))

    @pl.loop(0, NZ)
    def _(i):
        odd = lax.rem(i, 2)
        off = odd * ((i + 1) // 2) + (1 - odd) * lax.rem(NZ - i // 2, NZ)
        b = z_from(off)
        take(ga.at[b, :, pl.ds(0, NX - 1)], gx_r.at[b])
        for h in range(heads):
            prob = dot_t(v_ref[:, cols(h)], ga[b, h].reshape(block, HEAD))
            dp[h, b] = prob
            sb[b, pl.ds(3 * h + 2, 1)] = jnp.sum(w[h, b] * prob, axis=0, keepdims=True)

        @pl.when(i > 0)
        def _():
            stat_copy(NZ - off).start()

    for chain, (_, _, hops) in enumerate(CHAINS):
        if hops == NZ // 2:
            ring_step(chain, hops - 1)

    sz[z0] = sb[z0]
    take(but_one(sz), sz_r)

    def merged(ref):
        out = []
        for h in range(heads):
            tops = ref[:, 3 * h]
            top = jnp.max(tops, axis=0, keepdims=True)
            factor = jnp.exp2(tops - top)
            out += [
                top,
                jnp.sum(ref[:, 3 * h + 1] * factor, axis=0, keepdims=True),
                jnp.sum(ref[:, 3 * h + 2] * factor, axis=0, keepdims=True),
            ]
        return out

    pad = jnp.zeros((8 - 3 * heads, block), F32)
    sx[x0] = jnp.concatenate(merged(sz) + [pad], axis=0)

    def stat_x_copy(i):
        return remote(sx.at[x0], sx.at[x0], sx_s, sx_r, x_dev(i))

    each(NX, lambda i: stat_x_copy(i).start())
    for chain in range(len(CHAINS)):
        ring_step(chain, 2)
    take(but_one(sx), sx_r)

    whole = merged(sx)
    final = []
    for h in range(heads):
        top, total, product = whole[3 * h : 3 * h + 3]
        final += [top + jnp.log2(total), product / total]
    final.append(jnp.zeros((8 - len(final), block), F32))
    fin[z0] = jnp.concatenate(final, axis=0)

    def fin_copy(i):
        return remote(fin.at[z0], fin.at[z0], fz_s, fz_r, z_dev(i))

    each(NZ, lambda i: fin_copy(i).start())
    for chain in range(len(CHAINS)):
        ring_step(chain, 1)

    def nx_copy(i):
        return remote(nb.at[x_at(i)], nx.at[x0], nx_s, nx_r, x_dev(i))

    def dx_copy(b, i):
        return remote(db.at[b, x_at(i)], dx.at[b, x0], dx_s, dx_r.at[b], x_dev(i))

    def backward(first, last):
        @pl.loop(first, last)
        def _(i):
            b = z_from(i)

            for h in range(heads):
                factor = jnp.exp2(sb[b, pl.ds(3 * h, 1)] - fin[b, pl.ds(2 * h, 1)])
                weight = w[h, b] * factor
                low = weight.astype(BF16)
                grad = (weight * (dp[h, b] - fin[b, pl.ds(2 * h + 1, 1)])).astype(BF16)
                term = (dot(kt[h], grad) * SCALE).T.astype(BF16)
                db[b, :, h] = term.reshape(NX, rows, HEAD)
                gk_ref[:, cols(h)] += dot(grad, qa[b, h].reshape(block, HEAD))
                gv_ref[:, cols(h)] += dot(low, ga[b, h].reshape(block, HEAD))
            each(NX, lambda j: dx_copy(b, j).start())

    take(but_one(fin), fz_r)
    backward(0, NZ // 2)
    for h in range(heads):
        parts = [own_part(h, z0)]
        for chain, (head, _, _) in enumerate(CHAINS):
            if head == h:
                parts.append(arrived(chain, 1))
        total, level = joined(parts)
        total = total * jnp.exp2(level - fin[z0, pl.ds(2 * h, 1)])
        nb[:, h] = total.T.astype(BF16).reshape(NX, rows, HEAD)
    each(NX, lambda i: nx_copy(i).start())
    backward(NZ // 2, NZ)
    gk_ref[...] = gk_ref[...] * SCALE

    take(but_one(nx), nx_r)
    total = nb[x0].astype(F32)
    for j in range(1, NX):
        total += nx[x_at(j)].astype(F32)
    attended = total.astype(BF16)

    def pt_copy(i):
        return remote(pt.at[t_at(i)], pr.at[tp], pt_s, pt_r, t_dev(i))

    for t in range(NT):
        term = jnp.zeros((rows, width), F32)
        for h in range(heads):
            term += dot(attended[h], wout_ref[pl.ds(h * HEAD, HEAD), t * width : (t + 1) * width])
        pt[t] = term.astype(BF16)
    each(NT, lambda i: pt_copy(i).start())

    def dz_copy(i):
        return remote(ds.at[z_at(i)], dz.at[z0], dz_s, dz_r, z_dev(i))

    @pl.loop(0, NZ)
    def _(i):
        b = z_from(i)
        take(but_one(dx.at[b]), dx_r.at[b])
        total = db[b, x0].astype(F32)
        for j in range(1, NX):
            total += dx[b, x_at(j)].astype(F32)
        ds[b] = total.astype(BF16)

        @pl.when(i > 0)
        def _():
            dz_copy(NZ - i).start()

    take(but_one(pr), pt_r)
    pr[tp] = pt[tp]
    total = pr[0].astype(F32)
    for t in range(1, NT):
        total += pr[t].astype(F32)
    proj_ref[...] = total.astype(BF16)

    take(but_one(dz), dz_r)
    dz[z0] = ds[z0]
    total = dz[0].astype(F32)
    for j in range(1, NZ):
        total += dz[j].astype(F32)
    for h in range(heads):
        gq_ref[:, cols(h)] = total[h]

    sent(but_one(ct), ct_s)
    sent(but_one(pt), pt_s)
    sent(qa.at[0, :, pl.ds(0, NX - 1)], qx_s)
    sent(ga.at[pl.ds(0, NZ - 1), :, 0], gz_s)
    sent(ga.at[:, :, pl.ds(0, NX - 1)], gx_s)
    sent(but_one(sb), sz_s)
    sent(but_one(sx), sx_s)
    sent(but_one(fin), fz_s)
    sent(but_one(nb), nx_s)
    sent(db.at[:, pl.ds(0, NX - 1)], dx_s)
    sent(but_one(ds), dz_s)
    for h in range(heads):
        sent(qa.at[pl.ds(0, NZ - 1), h], qz_s.at[h])
        sent(ring_out.at[h, pl.ds(0, NZ - 1)], rn_s.at[h])


def hand_over(*refs):
    sems = refs[8]
    copies = [pltpu.make_async_copy(refs[i], refs[4 + i], sems.at[i]) for i in range(4)]
    for copy in copies:
        copy.start()
    for copy in copies:
        copy.wait()


def body(queries, keys, values, visible, out_weight, out_cotangent):
    rows, width = queries.shape
    ctx = keys.shape[0]
    heads = width // HEAD
    block = NX * rows
    vmem = pl.BlockSpec(memory_space=pltpu.VMEM)
    hbm = pl.BlockSpec(memory_space=pl.ANY)
    sem = pltpu.SemaphoreType.DMA
    outs = pl.pallas_call(
        kernel,
        out_shape=(
            pltpu.VMEM((rows, width), BF16),
            pltpu.VMEM((rows, width), F32),
            pltpu.VMEM((ctx, width), F32),
            pltpu.VMEM((ctx, width), F32),
        ),
        in_specs=[hbm] * 6,
        out_specs=[vmem] * 4,
        scratch_shapes=[
            pltpu.VMEM((ctx, width), BF16),
            pltpu.VMEM((ctx, width), BF16),
            pltpu.VMEM((NZ, 1, block), jnp.int32),
            pltpu.VMEM(out_weight.shape, BF16),
            sem((heads + 5,)),
            pltpu.VMEM((NZ, heads, NX, rows, HEAD), BF16),
            pltpu.VMEM((NZ, heads, NX, rows, HEAD), BF16),
            pltpu.VMEM((NT, rows, width), BF16),
            pltpu.VMEM((heads, HEAD, ctx), BF16),
            pltpu.VMEM((heads, HEAD, ctx), BF16),
            pltpu.VMEM((heads, NZ, ctx, block), F32),
            pltpu.VMEM((heads, NZ, ctx, block), F32),
            pltpu.VMEM((heads, NZ, HEAD, block), F32),
            pltpu.VMEM((NZ, 8, block), F32),
            pltpu.VMEM((NZ, 8, block), F32),
            pltpu.VMEM((NX, 8, block), F32),
            pltpu.VMEM((NZ, 8, block), F32),
            pltpu.VMEM((heads, NZ - 1, HEAD + LEVEL_ROWS, block), BF16),
            pltpu.VMEM((heads, NZ - 1, HEAD + LEVEL_ROWS, block), BF16),
            pltpu.VMEM((NX, heads, rows, HEAD), BF16),
            pltpu.VMEM((NX, heads, rows, HEAD), BF16),
            pltpu.VMEM((NZ, NX, heads, rows, HEAD), BF16),
            pltpu.VMEM((NZ, NX, heads, rows, HEAD), BF16),
            pltpu.VMEM((NZ, heads, rows, HEAD), BF16),
            pltpu.VMEM((NZ, heads, rows, HEAD), BF16),
            pltpu.VMEM((NT, rows, width), BF16),
            pltpu.VMEM((NT, rows, width), BF16),
            sem, sem,
            sem, sem, sem((heads,)), sem((len(CHAINS), NZ // 2)),
            sem, sem((NZ,)), sem, sem((NZ,)),
            sem, sem, sem, sem, sem, sem,
            sem((heads,)), sem((heads, NZ - 1)),
            sem, sem, sem, sem((NZ,)),
            sem, sem,
            sem, sem,
        ],
        compiler_params=pltpu.CompilerParams(
            collective_id=0, has_side_effects=True, vmem_limit_bytes=56 * 2**20
        ),
    )(queries, keys, values, visible.reshape(NZ, 1, block), out_weight, out_cotangent)
    return pl.pallas_call(
        hand_over,
        out_shape=tuple(jax.ShapeDtypeStruct(o.shape, o.dtype) for o in outs),
        in_specs=[vmem] * 4,
        out_specs=[hbm] * 4,
        scratch_shapes=[sem((4,))],
    )(*(pltpu.with_memory_space_constraint(o, pltpu.VMEM) for o in outs))


def solution(mesh):
    return jax.shard_map(
        body,
        mesh=mesh,
        in_specs=(
            P("seq", "tp"),
            P("seq", "tp"),
            P("seq", "tp"),
            P(),
            P("tp", None),
            P("seq", "tp"),
        ),
        out_specs=(P("seq", "tp"), P("seq", "tp"), P("seq", "tp"), P("seq", "tp")),
        check_vma=False,
    )
```

time: 86.2 us -> 70.9 us (0.82); the launches traced: 86 us -> 69.8 us
  Pallas kernels: 80.6 us -> 69.1 us
  local copies, waits for them, and re-layouts: 4.76 us -> 0 us
    pallas_call x1 -> x2, Pallas kernels: 80.6 us -> 69.1 us  [the longest x1 68.1 us: body(): pl.pallas_call(kernel, out_shape=(pltpu.VMEM((rows, width), BF16), pltpu....]
    unnamed x8 -> x0, local copies, waits for them, and re-layouts: 4.76 us -> none
where the time goes in v2:
time: 70.9 us; the launch traced here: 69.8 us
  Pallas kernels  69.1 us (97%)
    pallas_call x1, Pallas kernels, body(): pl.pallas_call(kernel, out_shape=(pltpu.VMEM((rows, width), BF16), pltpu....  68.1 us

profile of v2, /device:TPU:2, one launch (start us, length us, event | category | flops | bytes accessed | tf_op | source)
XLA Modules:
  0.0 69.8 jit_solution(4717313768482853448)
XLA Ops:
  0.6 68.1 %shard_map.93 = (bf16[64,256]{1,0:T(8,128)(2,1)S(1)}, f32[64,256]{1,0:T(8,128)S(1)}, f32[512,256]{1,0:T(8,128)S(1)}, f32[512,256]{1,0:T(8,128)S(1)}) custom-call(bf16[64,256]{1,0:T(8,128)(2,1)} %q_hbm.1, bf16[512,256]{1,0:T(8,128)(2,1)} %k_hbm.1, bf16[512,256]{1,0:T(8,128)(2,1)} %v_hbm.1, s32[8,1,256]{2,1,0:T(1,128)} %bitcast.1, bf16[256,2048]{1,0:T(8,128)(2,1)} %wout_hbm.1, ...), custom_call_target="tpu_custom_call" | custom-call | tf_op jit(solution)/shard_map/pallas_call | solution.py:432
  68.7 1.0 %shard_map.94 = (bf16[64,256]{1,0:T(8,128)(2,1)}, f32[64,256]{1,0:T(8,128)}, f32[512,256]{1,0:T(8,128)}, f32[512,256]{1,0:T(8,128)}) custom-call(bf16[64,256]{1,0:T(8,128)(2,1)S(1)} %get-tuple-element.8.refs_0_, f32[64,256]{1,0:T(8,128)S(1)} %get-tuple-element.9.refs_1_, f32[512,256]{1,0:T(8,128)S(1)} %get-tuple-element.10.refs_2_, ...), custom_call_target="tpu_custom_call" | custom-call | tf_op jit(solution)/shard_map/pallas_call | solution.py:483
